TPU v7x, 32 devices: a whole 2x2x4 slice. The times are simulated.
32 devices in a mesh: section: 4 (over x, core), seq: 8 (over z, y).
Axes of the slice: x: 2, y: 2, z: 4, core: 2. Of those that a mesh axis runs over, the one named last changes fastest.
Arguments:
- activations: bfloat16 [4, 2048, 1024], P('section', 'seq'), may hold values from -54 to 54
- cotangent: bfloat16 [4, 2048, 1024], P('section', 'seq'), may hold values from -6 to 6
- input_weights: bfloat16 [4, 1024, 3072], P('section'), may hold values from -3 to 3
- output_weights: bfloat16 [4, 1024, 1024], P('section'), may hold values from -0.1875 to 0.1875
- key_blocks: int32 [16, 4], P('seq'), may hold values from 0 to 15, as said below
- block_counts: int32 [16], P('seq'), may hold values from 1 to 4, as said below
Outputs:
- forward_out: bfloat16 [4, 2048, 1024], P('section', 'seq')
- backward_out: bfloat16 [4, 2048, 1024], P('section', 'seq')
Inputs may be any that keep to these rules, and one draw needn't show every extreme that they name: `key_blocks`: row b: slot 0 is b; slots 1 to block_counts[b] - 1 hold distinct blocks other than b, at most 2 blocks from b; later slots repeat b. `block_counts`: some block has 4 live slots and some has 1.
All inputs are finite; a program needn't handle non-finite values.
Results may differ from a plain program's by a relative error of at most 0.0036.
Values may be sent and summed in bfloat16 or wider, within the bound.
A program may use at most 128 MiB of HBM per device.

v0:
```python
import jax
import jax.numpy as jnp
from jax import lax
from jax.sharding import PartitionSpec as P

HEAD_DIM = 128
BLOCK = 128
REACH = 2


EPSILON = 1e-05


def shifted(value, axis, steps):
    count = lax.axis_size(axis)
    pairs = [(source, (source + steps) % count) for source in range(count)]
    return lax.ppermute(value, axis, pairs)


def with_halo(cells, sides, width):
    for axis, dim in sides:
        count = lax.axis_size(axis)
        ends = count - 1
        head = lax.slice_in_dim(cells, 0, width, axis=dim)
        tail = lax.slice_in_dim(cells, cells.shape[dim] - width, cells.shape[dim], axis=dim)
        cells = jnp.concatenate(
            [
                lax.ppermute(tail, axis, [(i, (i + 1) % count) for i in range(ends)]),
                cells,
                lax.ppermute(head, axis, [((i + 1) % count, i) for i in range(ends)]),
            ],
            axis=dim,
        )
    return cells


def block_scores(queries, key_rows):
    scaling = queries.shape[-1] ** (-0.5)
    return (
        jnp.einsum("hbqd,hbskd->hbqsk", queries, key_rows, preferred_element_type=jnp.float32)
        * scaling
    )


def live_mask(counts, slot_count):
    return jnp.arange(slot_count)[None, :] < counts[:, None]


def heads_first(rows, block_count, head_count):
    return rows.reshape(block_count, BLOCK, head_count, HEAD_DIM).transpose(2, 0, 1, 3)


def pairs_heads_first(rows, block_count, head_count):
    return rows.reshape(block_count, BLOCK, 2, head_count, HEAD_DIM).transpose(2, 3, 0, 1, 4)


def heads_to_rows(blocks):
    head_count, block_count, row_block, head_size = blocks.shape
    return blocks.transpose(1, 2, 0, 3).reshape(block_count * row_block, head_count * head_size)


def pairs_to_rows(blocks):
    pair_count, head_count, block_count, row_block, head_size = blocks.shape
    return blocks.transpose(2, 3, 0, 1, 4).reshape(
        block_count * row_block, pair_count * head_count * head_size
    )


def per_device(activations, cotangent, input_weights, output_weights, key_blocks, block_counts):
    arrived = shifted(activations[0], "section", 1)
    upstream = shifted(cotangent[0], "section", -1)
    weights_in = input_weights[0]
    weights_out = output_weights[0]
    feature_width = weights_out.shape[0]
    head_count = feature_width // HEAD_DIM
    row_count = arrived.shape[0]
    nblock = row_count // BLOCK
    slot_count = key_blocks.shape[1]
    scaling = HEAD_DIM ** (-0.5)
    span_blocks = nblock + 2 * REACH
    first_block = lax.axis_index("seq") * nblock
    values = arrived.astype(jnp.float32)
    factor = lax.rsqrt(jnp.mean(values * values, axis=-1, keepdims=True) + EPSILON)
    normed = values * factor
    projected = jnp.dot(
        normed.astype(jnp.bfloat16), weights_in, preferred_element_type=jnp.float32
    ).astype(jnp.bfloat16)
    queries = heads_first(projected[:, :feature_width], nblock, head_count)
    key_value = projected[:, feature_width:]
    margin = REACH * BLOCK
    widened = with_halo(key_value, (("seq", 0),), margin)
    window_pairs = pairs_heads_first(widened, span_blocks, head_count)
    window_index = key_blocks - first_block + REACH
    key_rows = window_pairs[0][:, window_index]
    value_rows = window_pairs[1][:, window_index]
    live_slots = live_mask(block_counts, slot_count)[None, :, None, :, None]
    scores = jnp.where(live_slots, block_scores(queries, key_rows), -1e30)
    row_max = jnp.max(scores, axis=(3, 4), keepdims=True)
    raw_weights = jnp.where(live_slots, jnp.exp(scores - row_max), 0.0)
    row_sum = jnp.sum(raw_weights, axis=(3, 4), keepdims=True)
    weights = raw_weights / row_sum
    weights_bf = weights.astype(jnp.bfloat16)
    attended = jnp.einsum(
        "hbqsk,hbskd->hbqd", weights_bf, value_rows, preferred_element_type=jnp.float32
    )
    attended = heads_to_rows(attended.astype(jnp.bfloat16))
    result = (values + jnp.dot(attended, weights_out, preferred_element_type=jnp.float32)).astype(
        jnp.bfloat16
    )
    attended_grad = jnp.einsum(
        "rd,wd->rw", upstream, weights_out, preferred_element_type=jnp.float32
    ).astype(jnp.bfloat16)
    grad_blocks = heads_first(attended_grad, nblock, head_count)
    weight_grad = jnp.einsum(
        "hbqd,hbskd->hbqsk", grad_blocks, value_rows, preferred_element_type=jnp.float32
    )
    weight_mean = jnp.sum(weights * weight_grad, axis=(3, 4), keepdims=True)
    score_grad = (weights * (weight_grad - weight_mean) * scaling).astype(jnp.bfloat16)
    query_grad = heads_to_rows(
        jnp.einsum("hbqsk,hbskd->hbqd", score_grad, key_rows, preferred_element_type=jnp.float32)
    )
    key_grad = jnp.einsum(
        "hbqsk,hbqd->hbskd", score_grad, queries, preferred_element_type=jnp.float32
    )
    value_grad = jnp.einsum(
        "hbqsk,hbqd->hbskd", weights_bf, grad_blocks, preferred_element_type=jnp.float32
    )
    grad_terms = jnp.stack([key_grad, value_grad]).reshape(
        2, head_count, nblock * slot_count, BLOCK, HEAD_DIM
    )
    placement = (window_index.reshape(-1)[:, None] == jnp.arange(span_blocks)[None, :]).astype(
        jnp.float32
    )
    window_sums = jnp.einsum(
        "ne,chnkd->chekd", placement, grad_terms, precision=lax.Precision.HIGHEST
    )
    window_rows = pairs_to_rows(window_sums)
    outgoing = jnp.concatenate([window_rows[:margin], window_rows[margin + row_count :]], axis=0)
    incoming = with_halo(outgoing.astype(jnp.bfloat16), (("seq", 0),), margin).astype(
        outgoing.dtype
    )
    owned_grads = window_rows[margin : margin + row_count]
    padding = jnp.zeros((row_count - margin, 2 * feature_width), jnp.float32)
    owned_grads = owned_grads + jnp.concatenate([incoming[:margin], padding], axis=0)
    owned_grads = owned_grads + jnp.concatenate([padding, incoming[3 * margin :]], axis=0)
    all_grads = jnp.concatenate([query_grad, owned_grads], axis=-1).astype(jnp.bfloat16)
    normed_grad = jnp.einsum("rc,dc->rd", all_grads, weights_in, preferred_element_type=jnp.float32)
    correction = jnp.mean(normed_grad * normed, axis=-1, keepdims=True)
    input_grad = (
        upstream.astype(jnp.float32) + factor * (normed_grad - normed * correction)
    ).astype(jnp.bfloat16)
    return (result[None], input_grad[None])


def solution(mesh):
    in_specs = (
        P("section", "seq", None),
        P("section", "seq", None),
        P("section", None, None),
        P("section", None, None),
        P("seq", None),
        P("seq"),
    )
    out_specs = (P("section", "seq", None), P("section", "seq", None))
    return jax.shard_map(
        per_device, mesh=mesh, in_specs=in_specs, out_specs=out_specs, check_vma=False
    )
```

profile of v0, /device:TPU:0, one launch (start us, length us, event | category | flops | bytes accessed | tf_op | source)
XLA Modules:
  0.0 178.7 jit_solution(15638323579001521958)
XLA Ops:
  0.6 0.0 copy-start
  0.6 0.5 collective-permute-start
  1.1 2.0 %collective-permute-start.3 = (bf16[256,1024]{1,0:T(8,128)(2,1)}, bf16[256,1024]{1,0:T(8,128)(2,1)S(1)}, u32[]{:S(2)}, u32[]{:S(2)}) collective-permute-start(bf16[256,1024]{1,0:T(8,128)(2,1)} %bitcast.143), channel_id=1, source_target_pairs={{0,24},{8,0},{16,8},{24,16},{1,25},{9,1},{17,9},{25,17},{2,26},{10... | collective-permute-start | bytes 1572872 | tf_op jit(solution)/shard_map/ppermute | solution.py:17
  3.1 10.0 %collective-permute-done = bf16[256,1024]{1,0:T(8,128)(2,1)S(1)} collective-permute-done((bf16[256,1024]{1,0:T(8,128)(2,1)}, bf16[256,1024]{1,0:T(8,128)(2,1)S(1)}, u32[]{:S(2)}, u32[]{:S(2)}) %collective-permute-start) | collective-permute-done | bytes 524320 | tf_op jit(solution)/shard_map/ppermute | solution.py:17
  13.1 0.2 fusion.52
  13.3 0.0 copy-start.15
  13.3 0.0 copy-start.16
  13.3 4.7 %fusion.8 = bf16[256,3072]{1,0:T(8,128)(2,1)S(1)} fusion(bf16[1,1024,3072]{2,1,0:T(8,128)(2,1)} %param.8, bf16[256,1024]{1,0:T(8,128)(2,1)S(1)} %collective-permute-done, f32[256]{0:T(256)S(1)} %add_rsqrt_fusion), kind=kOutput, calls=%fused_computation.14 | convolution fusion | flops 1612185600 | bytes 8389632 | tf_op jit(solution)/shard_map/dot_general | solution.py:85
  18.0 1.2 slice.57
  19.2 0.3 copy-done.11
  19.5 1.3 collective-permute-start.2
  20.8 6.7 %collective-permute-start.1 = (bf16[256,2048]{1,0:T(8,128)(2,1)}, bf16[256,2048]{1,0:T(8,128)(2,1)}, u32[]{:S(2)}, u32[]{:S(2)}) collective-permute-start(bf16[256,2048]{1,0:T(8,128)(2,1)} %slice.57), channel_id=1, source_target_pairs={{0,1},{1,2},{2,3},{3,4},{4,5},{5,6},{6,7},{8,9},{9,10},{10,11},{11... | collective-permute-start | bytes 3145736 | tf_op jit(solution)/shard_map/ppermute | solution.py:28
  27.5 0.1 eq.15
  27.5 0.1 reshape.75
  27.6 0.0 copy-done.16
  27.6 0.1 iota_compare_fusion.1
  27.7 0.0 collective-permute-done.3
  27.7 0.8 copy-done.13
  28.5 0.7 fusion.41
  29.3 0.1 copy.39
  29.4 1.1 slice_bitcast_fusion.2
  30.5 0.1 copy.36
  30.6 17.8 %collective-permute-done.2 = bf16[256,2048]{1,0:T(8,128)(2,1)} collective-permute-done((bf16[256,2048]{1,0:T(8,128)(2,1)}, bf16[256,2048]{1,0:T(8,128)(2,1)}, u32[]{:S(2)}, u32[]{:S(2)}) %collective-permute-start.2) | collective-permute-done | bytes 1048608 | tf_op jit(solution)/shard_map/ppermute | solution.py:30
  48.4 22.7 %collective-permute-done.1 = bf16[256,2048]{1,0:T(8,128)(2,1)} collective-permute-done((bf16[256,2048]{1,0:T(8,128)(2,1)}, bf16[256,2048]{1,0:T(8,128)(2,1)}, u32[]{:S(2)}, u32[]{:S(2)}) %collective-permute-start.1) | collective-permute-done | bytes 1048608 | tf_op jit(solution)/shard_map/ppermute | solution.py:28
  71.1 2.0 %maximum_bitcast_fusion = bf16[96,8,16,128]{3,1,2,0:T(8,128)(2,1)S(1)} fusion(bf16[256,2048]{1,0:T(8,128)(2,1)} %collective-permute-done.2, bf16[256,2048]{1,0:T(8,128)(2,1)} %slice.57, bf16[256,2048]{1,0:T(8,128)(2,1)} %collective-permute-done.1), kind=kLoop, calls=%fused_computation.17 | loop fusion | flops 9437184 | bytes 6291456
  73.1 1.0 copy.37
  74.1 2.4 %slice_bitcast_fusion.1 = (bf16[8,6,128,128]{3,0,2,1:T(8,128)(2,1)}, bf16[8,6,128,128]{3,0,2,1:T(8,128)(2,1)}) fusion(bf16[2,8,6,128,128]{4,1,0,3,2:T(8,128)(2,1)S(1)} %bitcast.131), kind=kLoop, calls=%fused_computation.28 | loop fusion | bytes 6291456 | tf_op jit(solution)/shard_map/squeeze | solution.py:94
  76.5 3.6 %gather_fusion = bf16[8,8,128,128]{3,1,2,0:T(8,128)(2,1)} fusion(bf16[8,6,128,128]{3,0,2,1:T(8,128)(2,1)} %get-tuple-element.4, s32[1024]{0:T(1024)S(1)} %pad_clamp_fusion), kind=kCustom, calls=%fused_computation | custom fusion | bytes 4194336 | tf_op jit(solution)/shard_map/gather | solution.py:94
  80.1 3.5 %copy.17 = bf16[8,8,128,128]{3,2,0,1:T(8,128)(2,1)} copy(bf16[8,8,128,128]{3,1,2,0:T(8,128)(2,1)} %gather_fusion) | data formatting | bytes 4194304 | tf_op jit(solution)/shard_map/gather | solution.py:94
  83.5 3.6 %gather_fusion.1 = bf16[8,8,128,128]{3,1,2,0:T(8,128)(2,1)} fusion(bf16[8,6,128,128]{3,0,2,1:T(8,128)(2,1)} %get-tuple-element.5, s32[1024]{0:T(1024)S(1)} %pad_clamp_fusion), kind=kCustom, calls=%fused_computation.1 | custom fusion | bytes 4194336 | tf_op jit(solution)/shard_map/gather | solution.py:95
  87.1 2.3 %copy.18 = bf16[8,8,128,128]{3,2,0,1:T(8,128)(2,1)S(1)} copy(bf16[8,8,128,128]{3,1,2,0:T(8,128)(2,1)} %gather_fusion.1) | data formatting | bytes 4194304 | tf_op jit(solution)/shard_map/gather | solution.py:95
  89.4 0.8 fusion.11
  90.2 0.0 copy-start.1
  90.2 1.1 fusion.16
  91.2 1.3 fusion.53
  92.5 1.8 %multiply_reduce_fusion = (f32[8,2,128]{2,1,0:T(2,128)S(1)}, f32[8,2,128,4,128]{2,4,3,1,0:T(8,128)S(1)}) fusion(f32[8,2,128]{2,1,0:T(2,128)S(1)} %fusion.16, f32[8,2,128]{2,1,0:T(2,128)S(1)} %get-tuple-element.8, f32[8,2,128,4,128]{2,4,3,1,0:T(8,128)S(1)} %get-tuple-element.9, pred[2,4]{1,0:T(4,128)(4,1)S(1)} %iota_compare_fusion.1, ...), kind=kOutput, calls=%fused_computation.11 | convolution fusion | flops 275773440 | bytes 11034632 | tf_op jit(solution)/shard_map/hbqd,hbskd->hbqsk/dot_general | solution.py:114
  94.3 2.4 %copy.25 = f32[1,8,8,128,128]{4,2,3,1,0:T(8,128)S(1)} copy(f32[1,8,8,128,128]{4,3,2,1,0:T(8,128)S(1)} %bitcast.134) | data formatting | bytes 8388608 | tf_op jit(solution)/shard_map/stack | solution.py:128
  96.7 1.7 multiply_convert_fusion
  98.4 0.7 fusion.63
  99.1 2.4 %copy.24 = f32[1,8,8,128,128]{4,2,3,1,0:T(8,128)S(1)} copy(f32[1,8,8,128,128]{4,3,2,1,0:T(8,128)S(1)} %bitcast.130) | data formatting | bytes 8388608 | tf_op jit(solution)/shard_map/stack | solution.py:128
  101.5 7.0 %fusion.80 = (bf16[6,128,2,8,128]{4,0,1,3,2:T(8,128)(2,1)S(1)}, f32[6,128,2,8,128]{4,0,1,3,2:T(8,128)}) fusion(s32[8]{0:T(128)S(1)} %eq.15, f32[1,8,8,128,128]{4,2,3,1,0:T(8,128)S(1)} %copy.25, f32[1,8,8,128,128]{4,2,3,1,0:T(8,128)S(1)} %copy.24), kind=kOutput, calls=%fused_computation.89 | convolution fusion | flops 154665008 | bytes 17825824 | tf_op jit(solution)/shard_map/ne,chnkd->chekd/dot_general | solution.py:134
  108.6 2.3 %fusion.79 = (bf16[2,128,2,8,128]{4,0,1,3,2:T(2,128)(2,1)S(1)}, bf16[2,128,2,8,128]{4,0,1,3,2:T(2,128)(2,1)}) fusion(bf16[6,128,2,8,128]{4,0,1,3,2:T(8,128)(2,1)S(1)} %get-tuple-element.12), kind=kLoop, calls=%fused_computation.88 | loop fusion | bytes 4194304 | tf_op jit(solution)/shard_map/slice | solution.py:138
  110.9 1.7 copy.27
  112.5 1.7 slice.47
  114.3 2.9 %copy.28 = bf16[2,128,2,8,128]{4,3,2,1,0:T(8,128)(2,1)} copy(bf16[2,128,2,8,128]{4,0,1,3,2:T(2,128)(2,1)} %get-tuple-element.3) | data formatting | bytes 2097152 | tf_op jit(solution)/shard_map/slice | solution.py:138
  117.2 2.3 %slice.49 = bf16[256,2048]{1,0:T(8,128)(2,1)} reshape(bf16[2,128,2,8,128]{4,3,2,1,0:T(8,128)(2,1)} %copy.28) | data formatting | bytes 2097152 | tf_op jit(solution)/shard_map/slice | solution.py:138
  119.5 1.5 collective-permute-start.5
  121.1 6.0 %collective-permute-start.4 = (bf16[256,2048]{1,0:T(8,128)(2,1)S(1)}, bf16[256,2048]{1,0:T(8,128)(2,1)}, u32[]{:S(2)}, u32[]{:S(2)}) collective-permute-start(bf16[256,2048]{1,0:T(8,128)(2,1)S(1)} %slice.47), channel_id=1, source_target_pairs={{0,1},{1,2},{2,3},{3,4},{4,5},{5,6},{6,7},{8,9},{9,10},{10,11},{11... | collective-permute-start | bytes 3145736 | tf_op jit(solution)/shard_map/ppermute | solution.py:28
  127.1 4.4 %fusion.40 = bf16[2,128,8,128]{3,1,0,2:T(8,128)(2,1)S(1)} fusion(bf16[8,2,4,128,128]{4,3,2,1,0:T(8,128)(2,1)} %bitcast.136, f32[8,2,128,4,128]{2,4,3,1,0:T(8,128)} %copy-done.1, f32[8,2,128]{2,1,0:T(2,128)S(1)} %fusion.16, f32[8,2,128]{2,1,0:T(2,128)S(1)} %get-tuple-element.8, pred[2,4]{1,0:T(4,128)(4,1)S(1)} %iota_compare_fusion.1), kind=kOutput, calls=%fused_computation.45 | convolution fusion | flops 274989056 | bytes 6832136 | tf_op jit(solution)/shard_map/hbqsk,hbskd->hbqd/dot_general | solution.py:103
  131.5 1.1 copy.20
  132.6 0.8 fusion.39
  133.4 0.3 copy.23
  133.7 0.9 copy.66
  134.7 4.5 %slice.60 = f32[2,128,2,8,128]{4,0,1,3,2:T(2,128)S(1)} slice(f32[6,128,2,8,128]{4,0,1,3,2:T(8,128)} %get-tuple-element.13), slice={[2:4], [0:128], [0:2], [0:8], [0:128]} | slice | bytes 4194304 | tf_op jit(solution)/shard_map/slice | solution.py:142
  139.1 2.5 %copy.26 = f32[2,128,2,8,128]{4,3,2,1,0:T(8,128)} copy(f32[2,128,2,8,128]{4,0,1,3,2:T(2,128)S(1)} %slice.60) | data formatting | bytes 4194304 | tf_op jit(solution)/shard_map/slice | solution.py:142
  141.7 2.7 %slice.45 = f32[256,2048]{1,0:T(8,128)} reshape(f32[2,128,2,8,128]{4,3,2,1,0:T(8,128)} %copy.26) | data formatting | bytes 4194304 | tf_op jit(solution)/shard_map/slice | solution.py:142
  144.4 2.9 %fusion.44 = bf16[1,256,1024]{2,1,0:T(8,128)(2,1)} fusion(bf16[1,1024,1024]{2,1,0:T(8,128)(2,1)S(1)} %copy-done, bf16[256,1024]{1,0:T(8,128)(2,1)} %copy-done.9, bf16[32,8,8,128]{3,2,1,0:T(8,128)(2,1)} %bitcast.141), kind=kOutput, calls=%fused_computation.47 | convolution fusion | flops 537657344 | bytes 3670016 | tf_op jit(solution)/shard_map/dot_general | solution.py:107
  147.3 0.7 collective-permute-done.5
  147.9 22.5 %collective-permute-done.4 = bf16[256,2048]{1,0:T(8,128)(2,1)} collective-permute-done((bf16[256,2048]{1,0:T(8,128)(2,1)S(1)}, bf16[256,2048]{1,0:T(8,128)(2,1)}, u32[]{:S(2)}, u32[]{:S(2)}) %collective-permute-start.4) | collective-permute-done | bytes 1048608 | tf_op jit(solution)/shard_map/ppermute | solution.py:28
  170.5 0.0 copy-done.6
  170.5 2.1 %fusion.18 = bf16[256,2048]{1,0:T(8,128)(2,1)S(1)} fusion(f32[256,2048]{1,0:T(8,128)S(1)} %copy-done.6, bf16[256,2048]{1,0:T(8,128)(2,1)} %collective-permute-done.5, bf16[256,2048]{1,0:T(8,128)(2,1)S(1)} %slice.47, bf16[256,2048]{1,0:T(8,128)(2,1)S(1)} %copy-done.7, bf16[256,2048]{1,0:T(8,128)(2,1)} %collective-permute-done.4), kind=kLoop, calls=%fused_computation.22 | loop fusion | flops 9961472 | bytes 7340032 | tf_op jit(solution)/shard_map/convert.1
  172.6 0.0 copy-done.10
  172.6 4.9 %fusion.47 = (f32[256]{0:T(256)S(1)}, f32[256,1024]{1,0:T(8,128)S(1)}) fusion(bf16[256,1024]{1,0:T(8,128)(2,1)S(1)} %copy-done.10, f32[256]{0:T(256)S(1)} %add_rsqrt_fusion, bf16[1,1024,3072]{2,1,0:T(8,128)(2,1)} %param.8, bf16[256,2048]{1,0:T(8,128)(2,1)S(1)} %fusion.18, bf16[256,1024]{1,0:T(8,128)(2,1)S(1)} %bitcast.140), kind=kOutput, calls=%fused_computation.48 | convolution fusion | flops 1614806784 | bytes 9439232 | tf_op jit(solution)/shard_map/rc,dc->rd/dot_general | solution.py:147
  177.6 1.1 fusion.56
  (29 shorter events, 0.1 us)
Async XLA Ops:
  0.6 27.9 %copy-start = (bf16[1,1024,1024]{2,1,0:T(8,128)(2,1)S(1)}, bf16[1,1024,1024]{2,1,0:T(8,128)(2,1)}, u32[]{:S(2)}) copy-start(bf16[1,1024,1024]{2,1,0:T(8,128)(2,1)} %param.9) | copy-start | bytes 6291460
  0.6 12.5 %collective-permute-start = (bf16[256,1024]{1,0:T(8,128)(2,1)}, bf16[256,1024]{1,0:T(8,128)(2,1)S(1)}, u32[]{:S(2)}, u32[]{:S(2)}) collective-permute-start(bf16[256,1024]{1,0:T(8,128)(2,1)} %bitcast.142), channel_id=1, source_target_pairs={{0,8},{8,16},{16,24},{24,0},{1,9},{9,17},{17,25},{25,1},{2,10},{10... | collective-permute-start | bytes 1572872 | tf_op jit(solution)/shard_map/ppermute | solution.py:17
  1.1 26.6 %collective-permute-start.3 = (bf16[256,1024]{1,0:T(8,128)(2,1)}, bf16[256,1024]{1,0:T(8,128)(2,1)S(1)}, u32[]{:S(2)}, u32[]{:S(2)}) collective-permute-start(bf16[256,1024]{1,0:T(8,128)(2,1)} %bitcast.143), channel_id=1, source_target_pairs={{0,24},{8,0},{16,8},{24,16},{1,25},{9,1},{17,9},{25,17},{2,26},{10... | collective-permute-start | bytes 1572872 | tf_op jit(solution)/shard_map/ppermute | solution.py:17
  13.1 4.9 %copy-start.9 = (bf16[256,1024]{1,0:T(8,128)(2,1)}, bf16[256,1024]{1,0:T(8,128)(2,1)S(1)}, u32[]{:S(2)}) copy-start(bf16[256,1024]{1,0:T(8,128)(2,1)S(1)} %collective-permute-done) | copy-start | bytes 1572868
  13.3 14.2 %copy-start.15 = (s32[2,4]{1,0:T(2,128)S(1)}, s32[2,4]{1,0:T(2,128)}, u32[]{:S(2)}) copy-start(s32[2,4]{1,0:T(2,128)} %param.10) | copy-start | bytes 100
  13.3 14.3 %copy-start.16 = (s32[2]{0:T(128)S(1)}, s32[2]{0:T(128)}, u32[]{:S(2)}) copy-start(s32[2]{0:T(128)} %param.11) | copy-start | bytes 28
  18.0 1.5 copy-start.11
  19.5 28.9 %collective-permute-start.2 = (bf16[256,2048]{1,0:T(8,128)(2,1)}, bf16[256,2048]{1,0:T(8,128)(2,1)}, u32[]{:S(2)}, u32[]{:S(2)}) collective-permute-start(bf16[256,2048]{1,0:T(8,128)(2,1)} %slice.57), channel_id=1, source_target_pairs={{1,0},{2,1},{3,2},{4,3},{5,4},{6,5},{7,6},{9,8},{10,9},{11,10},{12... | collective-permute-start | bytes 3145736 | tf_op jit(solution)/shard_map/ppermute | solution.py:30
  20.8 50.3 %collective-permute-start.1 = (bf16[256,2048]{1,0:T(8,128)(2,1)}, bf16[256,2048]{1,0:T(8,128)(2,1)}, u32[]{:S(2)}, u32[]{:S(2)}) collective-permute-start(bf16[256,2048]{1,0:T(8,128)(2,1)} %slice.57), channel_id=1, source_target_pairs={{0,1},{1,2},{2,3},{3,4},{4,5},{5,6},{6,7},{8,9},{9,10},{10,11},{11... | collective-permute-start | bytes 3145736 | tf_op jit(solution)/shard_map/ppermute | solution.py:28
  27.7 0.8 copy-start.13
  87.1 2.3 %copy-start.2 = (bf16[8,8,128,128]{3,2,0,1:T(8,128)(2,1)S(1)}, bf16[8,8,128,128]{3,2,0,1:T(8,128)(2,1)}, u32[]{:S(2)}) copy-start(bf16[8,8,128,128]{3,2,0,1:T(8,128)(2,1)} %copy.17) | copy-start | bytes 6291460
  89.3 3.2 %copy-start.8 = (bf16[8,8,128,128]{3,2,0,1:T(8,128)(2,1)}, bf16[8,8,128,128]{3,2,0,1:T(8,128)(2,1)S(1)}, u32[]{:S(2)}) copy-start(bf16[8,8,128,128]{3,2,0,1:T(8,128)(2,1)S(1)} %copy.18) | copy-start | bytes 6291460
  90.2 6.5 %copy-start.1 = (f32[8,2,128,4,128]{2,4,3,1,0:T(8,128)}, f32[8,2,128,4,128]{2,4,3,1,0:T(8,128)S(1)}, u32[]{:S(2)}) copy-start(f32[8,2,128,4,128]{2,4,3,1,0:T(8,128)S(1)} %get-tuple-element.9) | copy-start | bytes 12582916
  98.4 3.1 %copy-start.4 = (bf16[8,2,128,4,128]{2,4,3,1,0:T(8,128)(2,1)}, bf16[8,2,128,4,128]{2,4,3,1,0:T(8,128)(2,1)S(1)}, u32[]{:S(2)}) copy-start(bf16[8,2,128,4,128]{2,4,3,1,0:T(8,128)(2,1)S(1)} %multiply_convert_fusion) | copy-start | bytes 6291460
  119.5 13.1 %copy-start.3 = (bf16[8,8,128,128]{3,2,0,1:T(8,128)(2,1)S(1)}, bf16[8,8,128,128]{3,2,0,1:T(8,128)(2,1)}, u32[]{:S(2)}) copy-start(bf16[8,8,128,128]{3,2,0,1:T(8,128)(2,1)} %copy.17) | copy-start | bytes 6291460
  119.5 13.1 %copy-start.5 = (bf16[8,2,128,4,128]{2,4,3,1,0:T(8,128)(2,1)S(1)}, bf16[8,2,128,4,128]{2,4,3,1,0:T(8,128)(2,1)}, u32[]{:S(2)}) copy-start(bf16[8,2,128,4,128]{2,4,3,1,0:T(8,128)(2,1)} %copy-done.4) | copy-start | bytes 6291460
  119.5 28.4 %collective-permute-start.5 = (bf16[256,2048]{1,0:T(8,128)(2,1)}, bf16[256,2048]{1,0:T(8,128)(2,1)}, u32[]{:S(2)}, u32[]{:S(2)}) collective-permute-start(bf16[256,2048]{1,0:T(8,128)(2,1)} %slice.49), channel_id=1, source_target_pairs={{1,0},{2,1},{3,2},{4,3},{5,4},{6,5},{7,6},{9,8},{10,9},{11,10},{12... | collective-permute-start | bytes 3145736 | tf_op jit(solution)/shard_map/ppermute | solution.py:30
  121.1 49.4 %collective-permute-start.4 = (bf16[256,2048]{1,0:T(8,128)(2,1)S(1)}, bf16[256,2048]{1,0:T(8,128)(2,1)}, u32[]{:S(2)}, u32[]{:S(2)}) collective-permute-start(bf16[256,2048]{1,0:T(8,128)(2,1)S(1)} %slice.47), channel_id=1, source_target_pairs={{0,1},{1,2},{2,3},{3,4},{4,5},{5,6},{6,7},{8,9},{9,10},{10,11},{11... | collective-permute-start | bytes 3145736 | tf_op jit(solution)/shard_map/ppermute | solution.py:28
  144.4 26.1 %copy-start.6 = (f32[256,2048]{1,0:T(8,128)S(1)}, f32[256,2048]{1,0:T(8,128)}, u32[]{:S(2)}) copy-start(f32[256,2048]{1,0:T(8,128)} %slice.45) | copy-start | bytes 6291460
  144.4 26.1 %copy-start.7 = (bf16[256,2048]{1,0:T(8,128)(2,1)S(1)}, bf16[256,2048]{1,0:T(8,128)(2,1)}, u32[]{:S(2)}) copy-start(bf16[256,2048]{1,0:T(8,128)(2,1)} %slice.49) | copy-start | bytes 3145732
  147.3 25.3 %copy-start.10 = (bf16[256,1024]{1,0:T(8,128)(2,1)S(1)}, bf16[256,1024]{1,0:T(8,128)(2,1)}, u32[]{:S(2)}) copy-start(bf16[256,1024]{1,0:T(8,128)(2,1)} %copy-done.9) | copy-start | bytes 1572868
  147.3 25.3 %copy-start.12 = (bf16[32,8,8,128]{3,1,2,0:T(8,128)(2,1)S(1)}, bf16[32,8,8,128]{3,1,2,0:T(8,128)(2,1)}, u32[]{:S(2)}) copy-start(bf16[32,8,8,128]{3,1,2,0:T(8,128)(2,1)} %copy.66) | copy-start | bytes 1572868
  172.6 5.0 %copy-start.14 = (bf16[256,1024]{1,0:T(8,128)(2,1)S(1)}, bf16[256,1024]{1,0:T(8,128)(2,1)}, u32[]{:S(2)}) copy-start(bf16[256,1024]{1,0:T(8,128)(2,1)} %copy-done.13) | copy-start | bytes 1572868
where the time goes:
time: 179 us
  waiting for transfers between devices  73.6 us (41%)
  local copies, waits for them, and re-layouts  47.9 us (27%)
  matrix products  30 us (17%)
  starting transfers between devices  18 us (10%)
  other arithmetic  8.25 us (5%)
    ppermute x2, waiting for transfers between devices, with_halo(): lax.ppermute(tail, axis, [(i, (i + 1) % count) for i in range(ends)])  45.2 us
    ppermute x2, waiting for transfers between devices, with_halo(): lax.ppermute(head, axis, [((i + 1) % count, i) for i in range(ends)])  18.5 us
    ppermute x2, starting transfers between devices, with_halo(): lax.ppermute(tail, axis, [(i, (i + 1) % count) for i in range(ends)])  12.7 us
    ppermute x2, waiting for transfers between devices, shifted(): return lax.ppermute(value, axis, pairs)  9.97 us
    slice x3, local copies, waits for them, and re-layouts, per_device(): owned_grads = window_rows[margin:margin + row_count]  9.74 us
    dot_general x1, matrix products, per_device(): jnp.einsum('ne,chnkd->chekd', placement, grad_terms, precision=lax.Precis...  7.04 us
    gather x2, local copies, waits for them, and re-layouts, per_device(): key_rows = window_pairs[0][:, window_index]  7.01 us
    gather x2, local copies, waits for them, and re-layouts, per_device(): value_rows = window_pairs[1][:, window_index]  5.81 us
  transfers between devices with their start and end apart: 6, of which 5 were waited for; matrix products, arithmetic and copies ran while one was open for 16% of the time, Pallas kernels for 0%

commit v1 on v0

v1 whole, which is shorter than its diff:
```python
import functools

import jax
import jax.numpy as jnp
from jax import lax
from jax.experimental import pallas as pl
from jax.experimental.pallas import tpu as pltpu
from jax.sharding import PartitionSpec as P

HEAD_DIM = 128
BLOCK = 128
EPSILON = 1e-05
LOG2E = 1.4426950408889634
DEAD = -1e30
MESH = pl.DeviceIdType.MESH

NN = (((1,), (0,)), ((), ()))
NT = (((1,), (1,)), ((), ()))
TN = (((0,), (0,)), ((), ()))


def dot(a, b, dims):
    return lax.dot_general(a, b, dims, preferred_element_type=jnp.float32)


def kernel(
    n_section, n_seq, chunks,
    act, cot, w_in_hbm, w_out_hbm, key_blocks, counts,
    out_fwd, out_bwd,
    w_in, w_out, a_win, c_win, x_bf, qkv, grad_heads, attended, grads, key_grad, value_grad, normed_grad,
    stats, stats_win, w_sems, send_sems, recv_sems, stat_send, stat_recv,
):
    rows, width = act.shape
    heads = width // HEAD_DIM
    scaling = HEAD_DIM ** (-0.5)
    piece = rows // chunks
    slots = key_blocks.shape[1]

    s = lax.axis_index("section")
    q = lax.axis_index("seq")
    odd = lax.rem(q, 2)
    sgn = 1 - 2 * odd
    partner = q + sgn
    far = q - sgn
    z_to = q + 2 * sgn
    z_from = q - 2 * sgn
    has_to = jnp.logical_and(z_to >= 0, z_to < n_seq)
    has_far = jnp.logical_and(z_from >= 0, z_from < n_seq)
    up = lax.rem(s + 1, n_section)
    down = lax.rem(s + n_section - 1, n_section)

    loads = [
        pltpu.make_async_copy(w_in_hbm, w_in, w_sems.at[0]),
        pltpu.make_async_copy(w_out_hbm, w_out, w_sems.at[1]),
    ]
    for load in loads:
        load.start()

    barrier = pltpu.get_barrier_semaphore()

    def greet(section, seq):
        pl.semaphore_signal(barrier, inc=1, device_id=(section, seq), device_id_type=MESH)

    greet(up, q)
    greet(down, q)
    greet(s, partner)

    @pl.when(has_to)
    def _():
        greet(s, z_to)

    @pl.when(has_far)
    def _():
        greet(s, z_from)
        greet(s, far)

    pl.semaphore_wait(barrier, 3 + jnp.where(has_to, 1, 0) + jnp.where(has_far, 2, 0))

    def hop(kind, step, c):
        window = (a_win, c_win)[kind]
        part = pl.ds(c * piece, piece)
        if step == 0:
            src = (act, cot)[kind].at[part]
            target = ((up, down)[kind], q)
        elif step == 1:
            src = window.at[0, part]
            target = (s, partner)
        else:
            src = window.at[1, part]
            target = (s, z_to)
        return pltpu.make_async_remote_copy(
            src_ref=src,
            dst_ref=window.at[step, part],
            send_sem=send_sems.at[kind, step, c],
            recv_sem=recv_sems.at[kind, step, c],
            device_id=target,
            device_id_type=MESH,
        )

    def to_partner(kind, c):
        hop(kind, 0, c).wait_recv()
        hop(kind, 1, c).start()

    def to_far(kind, c):
        hop(kind, 1, c).wait_recv()

        @pl.when(has_to)
        def _():
            hop(kind, 2, c).start()

    for c in range(chunks):
        hop(0, 0, c).start()

    first = q * 2
    starts = (q * 2, partner * 2, far * 2)
    bias = []
    for i in range(2):
        line = []
        for slot in range(3):
            for j in range(2):
                wanted = starts[slot] + j
                found = jnp.float32(DEAD)
                for k in range(slots):
                    hit = jnp.logical_and(key_blocks[i, k] == wanted, counts[i] > k)
                    found = jnp.where(hit, jnp.float32(0.0), found)
                line.append(found)
        bias.append(line)
    lanes = lax.broadcasted_iota(jnp.int32, (1, rows), 1)
    for e in range(6):
        stats[pl.ds(16 + e, 1), :] = jnp.where(lanes < BLOCK, bias[0][e], bias[1][e])

    @pl.when(jnp.logical_not(has_far))
    def _():
        a_win[2] = jnp.zeros((rows, width), jnp.bfloat16)
        c_win[2] = jnp.zeros((rows, width), jnp.bfloat16)
        stats_win[1, 0:16, :] = jnp.zeros((16, rows), jnp.float32)
        stats_win[1, 16:24, :] = jnp.full((8, rows), DEAD, jnp.float32)

    def norm(slot):
        values = a_win[slot].astype(jnp.float32)
        factor = lax.rsqrt(jnp.mean(values * values, axis=-1, keepdims=True) + EPSILON)
        x_bf[...] = (values * factor).astype(jnp.bfloat16)

    tile = 512
    per = tile // HEAD_DIM

    def project(slot, low, high):
        def body(t, carry):
            col = pl.multiple_of(t * tile, tile)
            result = dot(x_bf[...], w_in[:, pl.ds(col, tile)], NN).astype(jnp.bfloat16)
            for i in range(per):
                qkv[t * per + i, slot * rows : (slot + 1) * rows, :] = result[:, i * HEAD_DIM : (i + 1) * HEAD_DIM]
            return carry

        lax.fori_loop(low, high, body, 0)

    def out_grad(slot):
        def body(t, carry):
            row = pl.multiple_of(t * tile, tile)
            result = dot(c_win[slot], w_out[pl.ds(row, tile), :], NT).astype(jnp.bfloat16)
            for i in range(per):
                grad_heads[t * per + i, slot * rows : (slot + 1) * rows, :] = result[:, i * HEAD_DIM : (i + 1) * HEAD_DIM]
            return carry

        lax.fori_loop(0, width // tile, body, 0)

    tiles = 3 * width // tile

    for c in range(chunks):
        to_partner(0, c)
    for c in range(chunks):
        hop(1, 0, c).start()
    norm(0)
    loads[0].wait()
    loads[1].wait()
    for c in range(chunks):
        project(0, tiles * c // chunks, tiles * (c + 1) // chunks)
        to_far(0, c)
    for c in range(chunks):
        to_partner(1, c)
    out_grad(0)
    norm(1)
    project(1, 0, tiles)

    @pl.when(has_far)
    def _():
        for c in range(chunks):
            hop(0, 2, c).wait_recv()

    norm(2)
    project(2, 0, tiles)

    def attend(h, carry):
        query = qkv[h, 0:rows, :]
        keys = qkv[heads + h]
        values = qkv[2 * heads + h]
        grad = grad_heads[h, 0:rows, :]
        raw = dot(keys, query, NT) * (scaling * LOG2E)
        raw = jnp.concatenate(
            [raw[e * BLOCK : (e + 1) * BLOCK] + stats[pl.ds(16 + e, 1), :] for e in range(6)], axis=0
        )
        top = jnp.max(raw, axis=0, keepdims=True)
        power = jnp.exp2(raw - top)
        total = jnp.sum(power, axis=0, keepdims=True)
        weights = power * (1.0 / total)
        weights_bf = weights.astype(jnp.bfloat16)
        column = pl.ds(pl.multiple_of(h * HEAD_DIM, HEAD_DIM), HEAD_DIM)
        attended[:, column] = dot(weights_bf, values, TN).astype(jnp.bfloat16)
        weight_grad = dot(values, grad, NT)
        mean = jnp.sum(weights * weight_grad, axis=0, keepdims=True)
        score_grad = (weights * (weight_grad - mean) * scaling).astype(jnp.bfloat16)
        grads[:, column] = dot(score_grad, keys, TN).astype(jnp.bfloat16)
        key_grad[h] = dot(score_grad[0:rows], query, NN)
        value_grad[h] = dot(weights_bf[0:rows], grad, NN)
        stats[pl.ds(h, 1), :] = top + jnp.log(total) * LOG2E
        stats[pl.ds(heads + h, 1), :] = mean
        return carry

    for c in range(chunks):
        lax.fori_loop(heads * c // chunks, heads * (c + 1) // chunks, attend, 0)
        to_far(1, c)

    def tell(slot):
        return pltpu.make_async_remote_copy(
            src_ref=stats,
            dst_ref=stats_win.at[slot - 1],
            send_sem=stat_send.at[slot - 1],
            recv_sem=stat_recv.at[slot - 1],
            device_id=(s, partner if slot == 1 else far),
            device_id_type=MESH,
        )

    tell(1).start()

    @pl.when(has_far)
    def _():
        tell(2).start()

    def forward(t, carry):
        column = pl.ds(pl.multiple_of(t * tile, tile), tile)
        result = dot(attended[...], w_out[:, column], NN)
        out_fwd[:, column] = (a_win[0, :, column].astype(jnp.float32) + result).astype(jnp.bfloat16)
        return carry

    lax.fori_loop(0, width // tile, forward, 0)

    def backward(part):
        def body(t, carry):
            there = pl.ds(pl.multiple_of(t * tile, tile), tile)
            term = dot(grads[:, part * width : (part + 1) * width], w_in[there, part * width : (part + 1) * width], NT)
            if part == 0:
                normed_grad[:, there] = term
            else:
                normed_grad[:, there] += term
            return carry

        lax.fori_loop(0, width // tile, body, 0)

    backward(0)

    def collect(slot):
        def body(h, carry):
            here = slice(slot * rows, (slot + 1) * rows)
            query = qkv[h, here, :]
            keys = qkv[heads + h, 0:rows, :]
            values = qkv[2 * heads + h, 0:rows, :]
            grad = grad_heads[h, here, :]
            level = stats_win[slot - 1, pl.ds(h, 1), :]
            mean = stats_win[slot - 1, pl.ds(heads + h, 1), :]
            raw = dot(keys, query, NT) * (scaling * LOG2E)
            weights = jnp.concatenate(
                [
                    jnp.exp2(raw[e * BLOCK : (e + 1) * BLOCK] + (stats_win[slot - 1, pl.ds(16 + 2 * slot + e, 1), :] - level))
                    for e in range(2)
                ],
                axis=0,
            )
            weight_grad = dot(values, grad, NT)
            score_grad = (weights * (weight_grad - mean) * scaling).astype(jnp.bfloat16)
            key_sum = key_grad[h] + dot(score_grad, query, NN)
            value_sum = value_grad[h] + dot(weights.astype(jnp.bfloat16), grad, NN)
            if slot == 1:
                key_grad[h] = key_sum
                value_grad[h] = value_sum
            else:
                grads[:, pl.ds(pl.multiple_of(width + h * HEAD_DIM, HEAD_DIM), HEAD_DIM)] = key_sum.astype(jnp.bfloat16)
                grads[:, pl.ds(pl.multiple_of(2 * width + h * HEAD_DIM, HEAD_DIM), HEAD_DIM)] = value_sum.astype(jnp.bfloat16)
            return carry

        lax.fori_loop(0, heads, body, 0)

    out_grad(1)
    tell(1).wait_recv()
    collect(1)

    @pl.when(has_far)
    def _():
        for c in range(chunks):
            hop(1, 2, c).wait_recv()
        tell(2).wait_recv()

    out_grad(2)
    collect(2)
    backward(1)
    backward(2)

    values = a_win[0].astype(jnp.float32)
    factor = lax.rsqrt(jnp.mean(values * values, axis=-1, keepdims=True) + EPSILON)
    normed = values * factor
    total_grad = normed_grad[...]
    correction = jnp.mean(total_grad * normed, axis=-1, keepdims=True)
    out_bwd[...] = (c_win[0].astype(jnp.float32) + factor * (total_grad - normed * correction)).astype(jnp.bfloat16)

    for kind in range(2):
        for c in range(chunks):
            hop(kind, 0, c).wait_send()
            hop(kind, 1, c).wait_send()
    tell(1).wait_send()

    @pl.when(has_to)
    def _():
        for kind in range(2):
            for c in range(chunks):
                hop(kind, 2, c).wait_send()

    @pl.when(has_far)
    def _():
        tell(2).wait_send()


def per_device(n_section, n_seq, activations, cotangent, input_weights, output_weights, key_blocks, block_counts):
    act, cot, w_in, w_out = activations[0], cotangent[0], input_weights[0], output_weights[0]
    rows, width = act.shape
    heads = width // HEAD_DIM
    chunks = 4
    bf, f32 = jnp.bfloat16, jnp.float32
    hbm = pl.BlockSpec(memory_space=pl.ANY)
    smem = pl.BlockSpec(memory_space=pltpu.SMEM)
    vmem = pl.BlockSpec(memory_space=pltpu.VMEM)
    fwd, bwd = pl.pallas_call(
        functools.partial(kernel, n_section, n_seq, chunks),
        out_shape=[jax.ShapeDtypeStruct((rows, width), bf)] * 2,
        in_specs=[hbm] * 4 + [smem] * 2,
        out_specs=[vmem] * 2,
        scratch_shapes=[
            pltpu.VMEM((width, 3 * width), bf),
            pltpu.VMEM((width, width), bf),
            pltpu.VMEM((3, rows, width), bf),
            pltpu.VMEM((3, rows, width), bf),
            pltpu.VMEM((rows, width), bf),
            pltpu.VMEM((3 * heads, 3 * rows, HEAD_DIM), bf),
            pltpu.VMEM((heads, 3 * rows, HEAD_DIM), bf),
            pltpu.VMEM((rows, width), bf),
            pltpu.VMEM((rows, 3 * width), bf),
            pltpu.VMEM((heads, rows, HEAD_DIM), f32),
            pltpu.VMEM((heads, rows, HEAD_DIM), f32),
            pltpu.VMEM((rows, width), f32),
            pltpu.VMEM((24, rows), f32),
            pltpu.VMEM((2, 24, rows), f32),
            pltpu.SemaphoreType.DMA((2,)),
            pltpu.SemaphoreType.DMA((2, 3, chunks)),
            pltpu.SemaphoreType.DMA((2, 3, chunks)),
            pltpu.SemaphoreType.DMA((2,)),
            pltpu.SemaphoreType.DMA((2,)),
        ],
        compiler_params=pltpu.CompilerParams(
            collective_id=0, has_side_effects=True, vmem_limit_bytes=56 * 2**20
        ),
    )(act, cot, w_in, w_out, key_blocks, block_counts)
    return fwd[None], bwd[None]


def solution(mesh):
    in_specs = (
        P("section", "seq", None),
        P("section", "seq", None),
        P("section", None, None),
        P("section", None, None),
        P("seq", None),
        P("seq"),
    )
    out_specs = (P("section", "seq", None), P("section", "seq", None))
    return jax.shard_map(
        functools.partial(per_device, mesh.shape["section"], mesh.shape["seq"]),
        mesh=mesh, in_specs=in_specs, out_specs=out_specs, check_vma=False,
    )
```

time: 179 us -> 58.4 us (0.33)
  waiting for transfers between devices: 73.6 us -> 0 us
  Pallas kernels: 0 us -> 53.8 us
  local copies, waits for them, and re-layouts: 47.9 us -> 3.74 us
  matrix products: 30 us -> 0 us
  starting transfers between devices: 18 us -> 0 us
  other arithmetic: 8.25 us -> 0 us
    ppermute x6 -> x0, waiting for transfers between devices: 73.6 us -> none  [the longest x2 45.2 us: with_halo(): lax.ppermute(tail, axis, [(i, (i + 1) % count) for i in range(ends)])]
    pallas_call x0 -> x1, Pallas kernels: none -> 53.8 us  [per_device(): pl.pallas_call(functools.partial(kernel, n_section, n_seq, chunks), out_s...]
    dot_general x11 -> x0, matrix products: 30 us -> none  [the longest x1 7.04 us: per_device(): jnp.einsum('ne,chnkd->chekd', placement, grad_terms, precision=lax.Precis...]
    slice x9 -> x0, local copies, waits for them, and re-layouts: 21.8 us -> none  [the longest x3 9.74 us: per_device(): owned_grads = window_rows[margin:margin + row_count]]
    ppermute x6 -> x0, starting transfers between devices: 18 us -> none  [the longest x2 12.7 us: with_halo(): lax.ppermute(tail, axis, [(i, (i + 1) % count) for i in range(ends)])]
    gather x4 -> x0, local copies, waits for them, and re-layouts: 12.8 us -> none  [the longest x2 7.01 us: per_device(): key_rows = window_pairs[0][:, window_index]]
    another operation x2 -> x0, local copies, waits for them, and re-layouts: 4.75 us -> none  [per_device(): jnp.stack([key_grad, value_grad])]
    squeeze x1 -> x0, local copies, waits for them, and re-layouts: 2.42 us -> none  [per_device(): key_rows = window_pairs[0][:, window_index]]
  transfers between devices with their start and end apart: 6 -> 0, of which waited for: 5 -> 0; matrix products, arithmetic and copies ran while one was open for 16% -> 0% of each run, Pallas kernels for 0% -> 0%
where the time goes in v1:
time: 58.4 us; the launch traced here: 58.2 us
  Pallas kernels  53.8 us (92%)
  local copies, waits for them, and re-layouts  3.74 us (6%)
  between operations  0.64 us (1%)
    pallas_call x1, Pallas kernels, per_device(): pl.pallas_call(functools.partial(kernel, n_section, n_seq, chunks), out_s...  53.8 us
    unnamed x2, local copies, waits for them, and re-layouts  3.74 us

profile of v1, /device:TPU:0, one launch (start us, length us, event | category | flops | bytes accessed | tf_op | source)
XLA Modules:
  0.0 58.2 jit_solution(13069909104504768502)
XLA Ops:
  0.6 53.8 %shard_map.77 = (bf16[256,1024]{1,0:T(8,128)(2,1)}, bf16[256,1024]{1,0:T(8,128)(2,1)}) custom-call(bf16[256,1024]{1,0:T(8,128)(2,1)} %bitcast.8, bf16[256,1024]{1,0:T(8,128)(2,1)} %bitcast.9, bf16[1024,3072]{1,0:T(8,128)(2,1)} %bitcast.6, bf16[1024,1024]{1,0:T(8,128)(2,1)} %bitcast.7, s32[2,4]{1,0:T(2,128)} %key_blocks.1, s32[2]{0:T(128)} %counts.1), custom_call_target="tpu_custom_call" | custom-call | tf_op jit(solution)/shard_map/pallas_call | solution.py:340
  54.4 1.9 %copy.10 = bf16[1,256,1024]{2,1,0:T(8,128)(2,1)} copy(bf16[1,256,1024]{2,1,0:T(8,128)(2,1)} %bitcast.11) | data formatting | bytes 1048576
  56.3 1.9 %copy.11 = bf16[1,256,1024]{2,1,0:T(8,128)(2,1)} copy(bf16[1,256,1024]{2,1,0:T(8,128)(2,1)} %bitcast.10) | data formatting | bytes 1048576

commit v2 on v1

--- a/solution.py
+++ b/solution.py
@@ -136,23 +136,19 @@
         stats_win[1, 0:16, :] = jnp.zeros((16, rows), jnp.float32)
         stats_win[1, 16:24, :] = jnp.full((8, rows), DEAD, jnp.float32)
 
-    def norm(slot):
-        values = a_win[slot].astype(jnp.float32)
+    def norm(slot, top, size):
+        values = a_win[slot, top : top + size].astype(jnp.float32)
         factor = lax.rsqrt(jnp.mean(values * values, axis=-1, keepdims=True) + EPSILON)
-        x_bf[...] = (values * factor).astype(jnp.bfloat16)
+        x_bf[top : top + size] = (values * factor).astype(jnp.bfloat16)
 
     tile = 512
     per = tile // HEAD_DIM
 
-    def project(slot, low, high):
-        def body(t, carry):
-            col = pl.multiple_of(t * tile, tile)
-            result = dot(x_bf[...], w_in[:, pl.ds(col, tile)], NN).astype(jnp.bfloat16)
+    def project(slot, top, size, low, high):
+        for t in range(low, high):
+            result = dot(x_bf[top : top + size], w_in[:, t * tile : (t + 1) * tile], NN).astype(jnp.bfloat16)
             for i in range(per):
-                qkv[t * per + i, slot * rows : (slot + 1) * rows, :] = result[:, i * HEAD_DIM : (i + 1) * HEAD_DIM]
-            return carry
-
-        lax.fori_loop(low, high, body, 0)
+                qkv[t * per + i, slot * rows + top : slot * rows + top + size, :] = result[:, i * HEAD_DIM : (i + 1) * HEAD_DIM]
 
     def out_grad(slot):
         def body(t, carry):
@@ -162,33 +158,46 @@
                 grad_heads[t * per + i, slot * rows : (slot + 1) * rows, :] = result[:, i * HEAD_DIM : (i + 1) * HEAD_DIM]
             return carry
 
-        lax.fori_loop(0, width // tile, body, 0)
+        lax.fori_loop(0, width // tile, body, 0, unroll=True)
 
     tiles = 3 * width // tile
+
+    def far_arrived(c):
+        @pl.when(has_far)
+        def _():
+            hop(0, 2, c).wait_recv()
 
     for c in range(chunks):
         to_partner(0, c)
     for c in range(chunks):
         hop(1, 0, c).start()
-    norm(0)
+    norm(0, 0, rows)
     loads[0].wait()
     loads[1].wait()
-    for c in range(chunks):
-        project(0, tiles * c // chunks, tiles * (c + 1) // chunks)
-        to_far(0, c)
-    for c in range(chunks):
-        to_partner(1, c)
+    project(0, 0, rows, 0, tiles // 2)
+    to_far(0, 0)
+    project(0, 0, rows, tiles // 2, tiles)
+    to_far(0, 1)
+    half = rows // 2
+    norm(1, 0, half)
+    project(1, 0, half, 0, tiles)
+    to_far(0, 2)
+    far_arrived(0)
+    far_arrived(1)
+    norm(2, 0, half)
+    project(2, 0, half, 0, tiles)
+    to_far(0, 3)
+    to_partner(1, 0)
+    to_partner(1, 1)
+    norm(1, half, half)
+    project(1, half, half, 0, tiles)
+    to_partner(1, 2)
+    to_partner(1, 3)
     out_grad(0)
-    norm(1)
-    project(1, 0, tiles)
-
-    @pl.when(has_far)
-    def _():
-        for c in range(chunks):
-            hop(0, 2, c).wait_recv()
-
-    norm(2)
-    project(2, 0, tiles)
+    far_arrived(2)
+    far_arrived(3)
+    norm(2, half, half)
+    project(2, half, half, 0, tiles)
 
     def attend(h, carry):
         query = qkv[h, 0:rows, :]
@@ -217,7 +226,7 @@
         return carry
 
     for c in range(chunks):
-        lax.fori_loop(heads * c // chunks, heads * (c + 1) // chunks, attend, 0)
+        lax.fori_loop(heads * c // chunks, heads * (c + 1) // chunks, attend, 0, unroll=2)
         to_far(1, c)
 
     def tell(slot):
@@ -242,7 +251,7 @@
         out_fwd[:, column] = (a_win[0, :, column].astype(jnp.float32) + result).astype(jnp.bfloat16)
         return carry
 
-    lax.fori_loop(0, width // tile, forward, 0)
+    lax.fori_loop(0, width // tile, forward, 0, unroll=True)
 
     def backward(part):
         def body(t, carry):
@@ -254,7 +263,7 @@
                 normed_grad[:, there] += term
             return carry
 
-        lax.fori_loop(0, width // tile, body, 0)
+        lax.fori_loop(0, width // tile, body, 0, unroll=True)
 
     backward(0)
 
@@ -287,7 +296,7 @@
                 grads[:, pl.ds(pl.multiple_of(2 * width + h * HEAD_DIM, HEAD_DIM), HEAD_DIM)] = value_sum.astype(jnp.bfloat16)
             return carry
 
-        lax.fori_loop(0, heads, body, 0)
+        lax.fori_loop(0, heads, body, 0, unroll=4)
 
     out_grad(1)
     tell(1).wait_recv()

time: 58.4 us -> 51.5 us (0.88)
  Pallas kernels: 53.8 us -> 46.9 us
    pallas_call x1, Pallas kernels: 53.8 us -> 46.9 us  [per_device(): pl.pallas_call(functools.partial(kernel, n_section, n_seq, chunks), out_s...]
where the time goes in v2:
time: 51.5 us; the launch traced here: 51.2 us
  Pallas kernels  46.9 us (91%)
  local copies, waits for them, and re-layouts  3.74 us (7%)
  between operations  0.64 us (1%)
    pallas_call x1, Pallas kernels, per_device(): pl.pallas_call(functools.partial(kernel, n_section, n_seq, chunks), out_s...  46.9 us
    unnamed x2, local copies, waits for them, and re-layouts  3.74 us

profile of v2, /device:TPU:0, one launch (start us, length us, event | category | flops | bytes accessed | tf_op | source)
XLA Modules:
  0.0 51.2 jit_solution(17527618938579009802)
XLA Ops:
  0.6 46.9 %shard_map.77 = (bf16[256,1024]{1,0:T(8,128)(2,1)}, bf16[256,1024]{1,0:T(8,128)(2,1)}) custom-call(bf16[256,1024]{1,0:T(8,128)(2,1)} %bitcast.8, bf16[256,1024]{1,0:T(8,128)(2,1)} %bitcast.9, bf16[1024,3072]{1,0:T(8,128)(2,1)} %bitcast.6, bf16[1024,1024]{1,0:T(8,128)(2,1)} %bitcast.7, s32[2,4]{1,0:T(2,128)} %key_blocks.1, s32[2]{0:T(128)} %counts.1), custom_call_target="tpu_custom_call" | custom-call | tf_op jit(solution)/shard_map/pallas_call | solution.py:349
  47.5 1.9 %copy.10 = bf16[1,256,1024]{2,1,0:T(8,128)(2,1)} copy(bf16[1,256,1024]{2,1,0:T(8,128)(2,1)} %bitcast.11) | data formatting | bytes 1048576
  49.4 1.9 %copy.11 = bf16[1,256,1024]{2,1,0:T(8,128)(2,1)} copy(bf16[1,256,1024]{2,1,0:T(8,128)(2,1)} %bitcast.10) | data formatting | bytes 1048576
